TPU v7x, 32 devices: a whole 2x2x4 slice. The times are simulated.
32 devices in a mesh: blk: 32 (over z, y, x, core).
Axes of the slice: x: 2, y: 2, z: 4, core: 2. Of those that a mesh axis runs over, the one named last changes fastest.
Arguments:
- blocks: float32 [4, 512, 256, 128], P(None, 'blk'), may hold values from -6 to 6
- first: float32 [512, 256], P('blk'), may hold values from -2.4 to 2.4
- second: float32 [8192, 256], P('blk'), may hold values from -2.4 to 2.4
- third: float32 [4096, 256], P('blk'), may hold values from -2.4 to 2.4
Outputs:
- first_final: float32 [512, 256], P('blk')
- second_final: float32 [8192, 256], P('blk')
- third_final: float32 [4096, 256], P('blk')
All inputs are finite; a program needn't handle non-finite values.
Results may differ from a plain program's by a relative error of at most 0.0003.
Values sent between devices are 32-bit elements; how exact they have to be, the bound alone decides.
A program may use at most 64 MiB of HBM per device.

v0:
```python
import functools

import jax
import jax.numpy as jnp
from jax import lax
from jax.experimental import pallas as pl
from jax.experimental.pallas import tpu as pltpu
from jax.sharding import PartitionSpec as P

momentum = 0.5
step_scale = 8.0
third_stride = 3
MESH = pl.DeviceIdType.MESH
NT = (((1,), (1,)), ((), ()))


def halves(x):
    high = x.astype(jnp.bfloat16)
    low = (x - high.astype(jnp.float32)).astype(jnp.bfloat16)
    return high, low


def dot(a, b):
    return jnp.dot(a, b, preferred_element_type=jnp.float32)


def kernel(
    count, strata, rates,
    blocks, first, second, third,
    first_out, second_out, third_out,
    target, rows_a, vel_a, grad_a, grad_c,
    recv_b, recv_c, send_b, send_c, past_b, past_c,
    keep_out_b, keep_out_c, keep_in_b, keep_in_c, last_b, last_c,
    cat_k, cat_r, pair_h, pair_l, miss, turn_h, turn_l,
    t_sem, b_sem, c_sem, pb_sem, pc_sem, kb_sem, kc_sem, lb_sem, lc_sem,
):
    rate_a, rate_b, rate_c = rates
    me = lax.axis_index("blk")
    i_rows = first.shape[0]
    j_rows, rank = second.shape
    k_rows = third.shape[0]
    wide = 2 * k_rows

    def other(by):
        return lax.rem(me + (by % count), count)

    def to(src, dst, sem, by):
        return pltpu.make_async_remote_copy(
            src_ref=src, dst_ref=dst, send_sem=sem.at[0], recv_sem=sem.at[1],
            device_id=(other(by),), device_id_type=MESH,
        )

    hops = set()
    for reach in (1, strata - 2, strata - 1):
        hops |= {reach, -reach, third_stride * reach, -third_stride * reach}
    hops = sorted(hops)
    barrier = pltpu.get_barrier_semaphore()
    for by in hops:
        pl.semaphore_signal(barrier, inc=1, device_id=(other(by),), device_id_type=MESH)
    loads = [
        pltpu.make_async_copy(blocks.at[s], target.at[s], t_sem.at[s]) for s in range(strata)
    ]
    for load in loads:
        load.start()
    pl.semaphore_wait(barrier, len(hops))

    rows_a[...] = first[...]
    sent = []
    for s in range(strata):
        if s == 0:
            b_ref, c_ref = second, third
        else:
            b_ref, c_ref = recv_b.at[s - 1], recv_c.at[s - 1]
            moved_c.wait_recv()
            moved_b.wait_recv()
        if s + 2 < strata:
            past = (
                to(c_ref, past_c.at[s], pc_sem.at[s], -third_stride),
                to(b_ref, past_b.at[s], pb_sem.at[s], -1),
            )
            for copy in past:
                copy.start()
            sent.extend(past)
        b_high, b_low = halves(b_ref[...])
        cat_k[...] = jnp.concatenate([b_high, b_high, b_low], axis=1)
        cat_r[...] = jnp.concatenate([b_high, b_high, b_low], axis=0)
        loads[s].wait()

        def model(p, _):
            c = c_ref[...]
            a0 = rows_a[pl.ds(2 * p, 1), :]
            a1 = rows_a[pl.ds(2 * p + 1, 1), :]
            high, low = halves(jnp.concatenate([c * a0, c * a1], axis=0))
            at = pl.multiple_of(p * wide, wide)
            pair_h[pl.ds(at, wide), :] = high
            pair_l[pl.ds(at, wide), :] = low
            made = lax.dot_general(
                cat_k[...], jnp.concatenate([high, low, high], axis=1), NT,
                preferred_element_type=jnp.float32,
            )
            want = jnp.concatenate([target[s, 2 * p], target[s, 2 * p + 1]], axis=1)
            high, low = halves(made - want)
            miss[pl.ds(0, j_rows), pl.ds(at, wide)] = high
            miss[pl.ds(j_rows, j_rows), pl.ds(at, wide)] = low
            turn_h[pl.ds(at, wide), :] = high.T
            turn_l[pl.ds(at, wide), :] = low.T
            return 0

        lax.fori_loop(0, i_rows // 2, model, 0, unroll=2)

        both = dot(miss[...], pair_h[...])
        grad = both[:j_rows] + both[j_rows:] + dot(miss[pl.ds(0, j_rows), :], pair_l[...])
        step_b = rate_b * grad
        if s + 1 == strata:
            send_b[s] = step_b
            moved_b = to(send_b.at[s], last_b, lb_sem, strata - 1)
            moved_b.start()
        else:
            now = b_ref[...]
            if s > 0:
                old_b.wait_recv()
                keep = momentum * (now - past_b[s - 1])
                now = now + keep
                vel = keep - step_b
            else:
                vel = -step_b
            now = now - step_b
            send_b[s] = now
            moved_b = to(send_b.at[s], recv_b.at[s], b_sem.at[s], -1)
            moved_b.start()
            if s + 2 == strata:
                keep_out_b[...] = now + momentum * vel
        sent.append(moved_b)

        grad_c[...] = jnp.zeros_like(grad_c)

        def spread(p, _):
            at = pl.multiple_of(p * wide, wide)
            high = turn_h[pl.ds(at, wide), :]
            low = turn_l[pl.ds(at, wide), :]
            d = dot(jnp.concatenate([high, low, high], axis=1), cat_r[...])
            c = c_ref[...]
            a0 = rows_a[pl.ds(2 * p, 1), :]
            a1 = rows_a[pl.ds(2 * p + 1, 1), :]
            grad_c[...] += a0 * d[:k_rows] + a1 * d[k_rows:]
            grad_a[pl.ds(2 * p, 1), :] = jnp.sum(c * d[:k_rows], axis=0, keepdims=True)
            grad_a[pl.ds(2 * p + 1, 1), :] = jnp.sum(c * d[k_rows:], axis=0, keepdims=True)
            return 0

        lax.fori_loop(0, i_rows // 2, spread, 0, unroll=2)

        step_c = rate_c * grad_c[...]
        if s + 1 == strata:
            send_c[s] = step_c
            moved_c = to(send_c.at[s], last_c, lc_sem, third_stride * (strata - 1))
            moved_c.start()
        else:
            now = c_ref[...]
            if s > 0:
                old_c.wait_recv()
                keep = momentum * (now - past_c[s - 1])
                now = now + keep
                vel = keep - step_c
            else:
                vel = -step_c
            now = now - step_c
            send_c[s] = now
            moved_c = to(send_c.at[s], recv_c.at[s], c_sem.at[s], -third_stride)
            moved_c.start()
            if s + 2 == strata:
                keep_out_c[...] = now + momentum * vel
                kept_b = to(keep_out_b, keep_in_b, kb_sem, strata - 2)
                kept_c = to(keep_out_c, keep_in_c, kc_sem, third_stride * (strata - 2))
                kept_b.start()
                kept_c.start()
                sent.extend([kept_b, kept_c])
        sent.append(moved_c)
        if s + 2 < strata:
            old_c, old_b = past

        step_a = rate_a * grad_a[...]
        if s == 0:
            rows_a[...] = rows_a[...] - step_a
            vel_a[...] = -step_a
        else:
            keep = momentum * vel_a[...]
            rows_a[...] = (rows_a[...] + keep) - step_a
            vel_a[...] = keep - step_a

    first_out[...] = rows_a[...]
    kept_b.wait_recv()
    moved_b.wait_recv()
    second_out[...] = keep_in_b[...] - last_b[...]
    kept_c.wait_recv()
    moved_c.wait_recv()
    third_out[...] = keep_in_c[...] - last_c[...]
    for copy in sent:
        copy.wait_send()


def shards(count, blocks, first, second, third):
    strata = blocks.shape[0]
    i_rows, rank = first.shape
    j_rows = second.shape[0]
    k_rows = third.shape[0]
    rates = (
        step_scale / (j_rows * k_rows),
        step_scale / (i_rows * k_rows),
        step_scale / (i_rows * j_rows),
    )
    f32, bf16 = jnp.float32, jnp.bfloat16
    a, b, c = (i_rows, rank), (j_rows, rank), (k_rows, rank)
    pairs = i_rows * k_rows
    vmem = pl.BlockSpec(memory_space=pltpu.VMEM)
    dma = pltpu.SemaphoreType.DMA
    return pl.pallas_call(
        functools.partial(kernel, count, strata, rates),
        out_shape=[jax.ShapeDtypeStruct(x, f32) for x in (a, b, c)],
        in_specs=[pl.BlockSpec(memory_space=pl.ANY), vmem, vmem, vmem],
        out_specs=[vmem, vmem, vmem],
        scratch_shapes=[
            pltpu.VMEM(blocks.shape, f32),
            pltpu.VMEM(a, f32), pltpu.VMEM(a, f32), pltpu.VMEM(a, f32), pltpu.VMEM(c, f32),
            pltpu.VMEM((strata - 1,) + b, f32), pltpu.VMEM((strata - 1,) + c, f32),
            pltpu.VMEM((strata,) + b, f32), pltpu.VMEM((strata,) + c, f32),
            pltpu.VMEM((strata - 2,) + b, f32), pltpu.VMEM((strata - 2,) + c, f32),
            pltpu.VMEM(b, f32), pltpu.VMEM(c, f32),
            pltpu.VMEM(b, f32), pltpu.VMEM(c, f32),
            pltpu.VMEM(b, f32), pltpu.VMEM(c, f32),
            pltpu.VMEM((j_rows, 3 * rank), bf16), pltpu.VMEM((3 * j_rows, rank), bf16),
            pltpu.VMEM((pairs, rank), bf16), pltpu.VMEM((pairs, rank), bf16),
            pltpu.VMEM((2 * j_rows, pairs), bf16),
            pltpu.VMEM((pairs, j_rows), bf16), pltpu.VMEM((pairs, j_rows), bf16),
            dma((strata,)),
            dma((strata - 1, 2)), dma((strata - 1, 2)),
            dma((strata - 2, 2)), dma((strata - 2, 2)),
            dma((2,)), dma((2,)), dma((2,)), dma((2,)),
        ],
        compiler_params=pltpu.CompilerParams(
            collective_id=0, has_side_effects=True, vmem_limit_bytes=48 * 1024 * 1024,
        ),
        cost_estimate=pl.CostEstimate(
            flops=strata * 18 * pairs * j_rows * rank,
            bytes_accessed=4 * strata * i_rows * j_rows * k_rows, transcendentals=0,
        ),
    )(blocks, first, second, third)


def solution(mesh):
    return jax.shard_map(
        functools.partial(shards, mesh.shape["blk"]),
        mesh=mesh,
        in_specs=(P(None, "blk", None, None), P("blk", None), P("blk", None), P("blk", None)),
        out_specs=(P("blk", None), P("blk", None), P("blk", None)),
        check_vma=False,
    )
```

profile of v0, /device:TPU:0, one launch (start us, length us, event | category | flops | bytes accessed | tf_op | source)
XLA Modules:
  0.0 66.7 jit_solution(13511283680226768456)
XLA Ops:
  0.6 0.0 copy-start
  0.6 0.9 %copy-done = f32[256,256]{1,0:T(8,128)S(1)} copy-done((f32[256,256]{1,0:T(8,128)S(1)}, f32[256,256]{1,0:T(8,128)}, u32[]{:S(2)}) %copy-start) | copy-done | bytes 262168
  1.6 0.0 copy-start.1
  1.6 0.9 %copy-done.1 = f32[128,256]{1,0:T(8,128)S(1)} copy-done((f32[128,256]{1,0:T(8,128)S(1)}, f32[128,256]{1,0:T(8,128)}, u32[]{:S(2)}) %copy-start.1) | copy-done | bytes 131096
  2.5 0.0 copy-start.2
  2.5 0.7 %copy-done.2 = f32[16,256]{1,0:T(8,128)S(1)} copy-done((f32[16,256]{1,0:T(8,128)S(1)}, f32[16,256]{1,0:T(8,128)}, u32[]{:S(2)}) %copy-start.2) | copy-done | bytes 16408
  3.2 61.5 %shard_map.67 = (f32[16,256]{1,0:T(8,128)S(1)}, f32[256,256]{1,0:T(8,128)S(1)}, f32[128,256]{1,0:T(8,128)S(1)}) custom-call(f32[4,16,256,128]{3,2,1,0:T(8,128)} %blocks.1, f32[16,256]{1,0:T(8,128)S(1)} %copy-done.2, f32[256,256]{1,0:T(8,128)S(1)} %copy-done, f32[128,256]{1,0:T(8,128)S(1)} %copy-done.1), custom_call_target="tpu_custom_call" | custom-call | flops 9663676416 | bytes 8388608 | tf_op jit(solution)/shard_map/pallas_call | solution.py:216
  64.8 0.6 copy.10
  65.4 0.7 %copy.11 = f32[256,256]{1,0:T(8,128)} copy(f32[256,256]{1,0:T(8,128)S(1)} %get-tuple-element.7) | data formatting | bytes 524288
  66.1 0.7 copy.12
Async XLA Ops:
  0.6 1.0 %copy-start = (f32[256,256]{1,0:T(8,128)S(1)}, f32[256,256]{1,0:T(8,128)}, u32[]{:S(2)}) copy-start(f32[256,256]{1,0:T(8,128)} %second.1) | copy-start | bytes 786436
  1.6 0.9 %copy-start.1 = (f32[128,256]{1,0:T(8,128)S(1)}, f32[128,256]{1,0:T(8,128)}, u32[]{:S(2)}) copy-start(f32[128,256]{1,0:T(8,128)} %third.1) | copy-start | bytes 393220
  2.5 0.7 %copy-start.2 = (f32[16,256]{1,0:T(8,128)S(1)}, f32[16,256]{1,0:T(8,128)}, u32[]{:S(2)}) copy-start(f32[16,256]{1,0:T(8,128)} %first.1) | copy-start | bytes 49156
where the time goes:
time: 66.9 us; the launch traced here: 66.7 us
  Pallas kernels  61.5 us (92%)
  local copies, waits for them, and re-layouts  4.53 us (7%)
    pallas_call x1, Pallas kernels, shards(): pl.pallas_call(functools.partial(kernel, count, strata, rates), out_shape...  61.5 us
    unnamed x9, local copies, waits for them, and re-layouts  4.53 us

commit v1 on v0

--- a/solution.py
+++ b/solution.py
@@ -62,7 +62,6 @@
     ]
     for load in loads:
         load.start()
-    pl.semaphore_wait(barrier, len(hops))
 
     rows_a[...] = first[...]
     sent = []
@@ -78,8 +77,9 @@
                 to(c_ref, past_c.at[s], pc_sem.at[s], -third_stride),
                 to(b_ref, past_b.at[s], pb_sem.at[s], -1),
             )
-            for copy in past:
-                copy.start()
+            if s > 0 and not False:
+                for copy in past:
+                    copy.start()
             sent.extend(past)
         b_high, b_low = halves(b_ref[...])
         cat_k[...] = jnp.concatenate([b_high, b_high, b_low], axis=1)
@@ -106,11 +106,13 @@
             turn_l[pl.ds(at, wide), :] = low.T
             return 0
 
-        lax.fori_loop(0, i_rows // 2, model, 0, unroll=2)
+        lax.fori_loop(0, i_rows // 2, model, 0, unroll=8)
 
         both = dot(miss[...], pair_h[...])
         grad = both[:j_rows] + both[j_rows:] + dot(miss[pl.ds(0, j_rows), :], pair_l[...])
         step_b = rate_b * grad
+        if s == 0:
+            pl.semaphore_wait(barrier, len(hops))
         if s + 1 == strata:
             send_b[s] = step_b
             moved_b = to(send_b.at[s], last_b, lb_sem, strata - 1)
@@ -147,7 +149,7 @@
             grad_a[pl.ds(2 * p + 1, 1), :] = jnp.sum(c * d[k_rows:], axis=0, keepdims=True)
             return 0
 
-        lax.fori_loop(0, i_rows // 2, spread, 0, unroll=2)
+        lax.fori_loop(0, i_rows // 2, spread, 0, unroll=8)
 
         step_c = rate_c * grad_c[...]
         if s + 1 == strata:
@@ -176,6 +178,9 @@
                 sent.extend([kept_b, kept_c])
         sent.append(moved_c)
         if s + 2 < strata:
+            if s == 0 or False:
+                for copy in past:
+                    copy.start()
             old_c, old_b = past
 
         step_a = rate_a * grad_a[...]

time: 66.9 us -> 64.7 us (0.967)
  Pallas kernels: 61.5 us -> 59.3 us
    pallas_call x1, Pallas kernels: 61.5 us -> 59.3 us  [shards(): pl.pallas_call(functools.partial(kernel, count, strata, rates), out_shape...]
where the time goes in v1:
time: 64.7 us; the launch traced here: 64.5 us
  Pallas kernels  59.3 us (92%)
  local copies, waits for them, and re-layouts  4.53 us (7%)
  between operations  0.65 us (1%)
    pallas_call x1, Pallas kernels, shards(): pl.pallas_call(functools.partial(kernel, count, strata, rates), out_shape...  59.3 us
    unnamed x9, local copies, waits for them, and re-layouts  4.53 us

profile of v1, /device:TPU:0, one launch (start us, length us, event | category | flops | bytes accessed | tf_op | source)
XLA Modules:
  0.0 64.5 jit_solution(7553939081781072386)
XLA Ops:
  0.6 0.0 copy-start
  0.6 0.9 %copy-done = f32[256,256]{1,0:T(8,128)S(1)} copy-done((f32[256,256]{1,0:T(8,128)S(1)}, f32[256,256]{1,0:T(8,128)}, u32[]{:S(2)}) %copy-start) | copy-done | bytes 262168
  1.6 0.0 copy-start.1
  1.6 0.9 %copy-done.1 = f32[128,256]{1,0:T(8,128)S(1)} copy-done((f32[128,256]{1,0:T(8,128)S(1)}, f32[128,256]{1,0:T(8,128)}, u32[]{:S(2)}) %copy-start.1) | copy-done | bytes 131096
  2.5 0.0 copy-start.2
  2.5 0.7 %copy-done.2 = f32[16,256]{1,0:T(8,128)S(1)} copy-done((f32[16,256]{1,0:T(8,128)S(1)}, f32[16,256]{1,0:T(8,128)}, u32[]{:S(2)}) %copy-start.2) | copy-done | bytes 16408
  3.2 59.3 %shard_map.67 = (f32[16,256]{1,0:T(8,128)S(1)}, f32[256,256]{1,0:T(8,128)S(1)}, f32[128,256]{1,0:T(8,128)S(1)}) custom-call(f32[4,16,256,128]{3,2,1,0:T(8,128)} %blocks.1, f32[16,256]{1,0:T(8,128)S(1)} %copy-done.2, f32[256,256]{1,0:T(8,128)S(1)} %copy-done, f32[128,256]{1,0:T(8,128)S(1)} %copy-done.1), custom_call_target="tpu_custom_call" | custom-call | flops 9663676416 | bytes 8388608 | tf_op jit(solution)/shard_map/pallas_call | solution.py:221
  62.5 0.6 copy.10
  63.1 0.7 %copy.11 = f32[256,256]{1,0:T(8,128)} copy(f32[256,256]{1,0:T(8,128)S(1)} %get-tuple-element.7) | data formatting | bytes 524288
  63.8 0.7 %copy.12 = f32[128,256]{1,0:T(8,128)} copy(f32[128,256]{1,0:T(8,128)S(1)} %get-tuple-element.8) | data formatting | bytes 262144
Async XLA Ops:
  0.6 1.0 %copy-start = (f32[256,256]{1,0:T(8,128)S(1)}, f32[256,256]{1,0:T(8,128)}, u32[]{:S(2)}) copy-start(f32[256,256]{1,0:T(8,128)} %second.1) | copy-start | bytes 786436
  1.6 0.9 %copy-start.1 = (f32[128,256]{1,0:T(8,128)S(1)}, f32[128,256]{1,0:T(8,128)}, u32[]{:S(2)}) copy-start(f32[128,256]{1,0:T(8,128)} %third.1) | copy-start | bytes 393220
  2.5 0.7 %copy-start.2 = (f32[16,256]{1,0:T(8,128)S(1)}, f32[16,256]{1,0:T(8,128)}, u32[]{:S(2)}) copy-start(f32[16,256]{1,0:T(8,128)} %first.1) | copy-start | bytes 49156
